TPU v7x, 32 devices: a whole 2x2x4 slice. The times are simulated.
32 devices in a mesh: row: 4 (over x, core), col: 8 (over z, y).
Axes of the slice: x: 2, y: 2, z: 4, core: 2. Of those that a mesh axis runs over, the one named last changes fastest.
Arguments:
- features: bfloat16 [4096, 256], P(('row', 'col')), may hold values from -6 to 6
- blocks: bfloat16 [32, 32, 128, 128], P('row', 'col'), may hold values from -0.09375 to 0.09375
- block_col: int32 [32, 32], P('row', 'col'), may hold values from 0 to 3
- row_count: int32 [32, 8], P('row', 'col'), may hold values from 0 to 4, as said below
- weight: bfloat16 [256, 256], replicated, may hold values from -0.375 to 0.375
- out_bias: float32 [256], replicated, may hold values from -4 to 4
Outputs:
- layer_out: bfloat16 [4096, 256], P(('row', 'col'))
Inputs may be any that keep to these rules, and one draw needn't show every extreme that they name: row_count[i, j] is how many of the 4 slots of block row i in column group j are in use; the others are ignored.
All inputs are finite; a program needn't handle non-finite values.
Results may differ from a plain program's by a relative error of at most 0.018.
Values may be sent and summed in bfloat16 or wider, within the bound.
A program may use at most 64 MiB of HBM per device.

v0:
```python
import jax
import jax.numpy as jnp
from jax import lax
from jax.sharding import PartitionSpec as P


def local_terms(blocks, block_col, counts, stripe):
    slot_ids = jnp.arange(block_col.shape[1], dtype=jnp.int32)[None, :]
    live_slots = (slot_ids < counts).astype(stripe.dtype)
    picked = stripe[block_col] * live_slots[:, :, None, None]
    term_rows = jnp.einsum("ikab,ikbf->iaf", blocks, picked, preferred_element_type=jnp.float32)
    return term_rows.reshape(-1, stripe.shape[2])


def local(features, blocks, block_col, row_count, weight, out_bias):
    feat_width = features.shape[1]
    block_size = blocks.shape[2]
    gathered = lax.all_gather(features, "row", axis=0, tiled=True)
    stripe = gathered.reshape(-1, block_size, feat_width)
    partial_value = local_terms(blocks, block_col, row_count, stripe)
    summed = lax.psum_scatter(
        partial_value.astype(jnp.bfloat16), "col", scatter_dimension=0, tiled=True
    )
    hidden = jnp.dot(summed, weight, preferred_element_type=jnp.float32) + out_bias
    return jnp.maximum(hidden, 0.0).astype(jnp.bfloat16)


def solution(mesh):
    return jax.shard_map(
        local,
        mesh=mesh,
        in_specs=(
            P(("row", "col"), None),
            P("row", "col", None, None),
            P("row", "col"),
            P("row", "col"),
            P(),
            P(),
        ),
        out_specs=P(("row", "col"), None),
        check_vma=False,
    )
```

profile of v0, /device:TPU:0, one launch (start us, length us, event | category | flops | bytes accessed | tf_op | source)
XLA Modules:
  0.0 89.6 jit_solution(6453641456935252513)
XLA Ops:
  6.5 0.0 copy-start
  6.5 0.0 reduce-scatter.2.cloned.1.call-start
  6.5 0.8 compare_select_fusion
  7.3 0.1 copy.8
  7.4 0.1 reshape.32
  7.5 0.7 fusion.11
  8.2 7.4 %all_gather.3 = bf16[512,256]{1,0:T(8,128)(2,1)S(1)} all-gather(bf16[128,256]{1,0:T(8,128)(2,1)} %param.6), channel_id=1, replica_groups=mesh['row'=4,'col'=8] {'row'}, dimensions={0}, use_global_device_ids=true | all-gather | bytes 327680 | tf_op jit(solution)/shard_map/all_gather | solution.py:18
  15.6 0.7 gather_fusion
  16.3 0.0 copy-done
  16.3 0.0 copy-start.1
  16.3 0.0 copy-start.2
  16.3 1.4 %fusion.5 = bf16[8,256,128]{1,2,0:T(8,128)(2,1)} fusion(bf16[8,4,128,128]{3,2,1,0:T(8,128)(2,1)S(1)} %copy-done, bf16[8,4,128,256]{3,2,1,0:T(8,128)(2,1)S(1)} %bitcast.15, bf16[8,4]{1,0:T(8,128)(2,1)S(1)} %fusion.11), kind=kOutput, calls=%fused_computation.4 | convolution fusion | flops 272891904 | bytes 3670080 | tf_op jit(solution)/shard_map/ikab,ikbf->iaf/dot_general | solution.py:11
  17.7 0.0 reduce-scatter.2.cloned.1.call-update
  17.8 63.4 %reduce-scatter.2.cloned.1.call-done = bf16[128,256]{1,0:T(8,128)(2,1)} async-done(((bf16[1024,256]{1,0:T(8,128)(2,1)}), bf16[128,256]{1,0:T(8,128)(2,1)}) %reduce-scatter.2.cloned.1.call-update) | async-done | bytes 65552 | tf_op jit(solution)/shard_map/reduce_scatter | solution.py:21
  81.1 0.0 copy-done.1
  81.1 0.0 copy-done.2
  81.1 1.6 %fusion.9 = bf16[128,256]{1,0:T(8,128)(2,1)} fusion(bf16[128,256]{1,0:T(8,128)(2,1)} %reduce-scatter.2.cloned.1.call-done, bf16[256,256]{1,0:T(8,128)(2,1)S(1)} %copy-done.1, f32[256]{0:T(256)S(1)} %copy-done.2), kind=kOutput, calls=%fused_computation.7 | convolution fusion | flops 16875520 | bytes 263168 | tf_op jit(solution)/shard_map/dot_general | solution.py:24
  (1 shorter events, 0.0 us)
Async XLA Ops:
  6.5 9.8 %copy-start = (bf16[8,4,128,128]{3,2,1,0:T(8,128)(2,1)S(1)}, bf16[8,4,128,128]{3,2,1,0:T(8,128)(2,1)}, u32[]{:S(2)}) copy-start(bf16[8,4,128,128]{3,2,1,0:T(8,128)(2,1)} %param.7) | copy-start | bytes 3145732
  6.5 74.6 %reduce-scatter.2.cloned.1.call-start = ((), (), s32[]{:S(2)}) async-start(), calls=%async_computation.1 | async-start | bytes 589824 | tf_op jit(solution)/shard_map/reduce_scatter | solution.py:21
  16.3 64.8 %copy-start.1 = (bf16[256,256]{1,0:T(8,128)(2,1)S(1)}, bf16[256,256]{1,0:T(8,128)(2,1)}, u32[]{:S(2)}) copy-start(bf16[256,256]{1,0:T(8,128)(2,1)} %param.10) | copy-start | bytes 393220
  16.3 64.8 %copy-start.2 = (f32[256]{0:T(256)S(1)}, f32[256]{0:T(256)}, u32[]{:S(2)}) copy-start(f32[256]{0:T(256)} %param.11) | copy-start | bytes 3076
Sparse Core Ops, SparseCore 0:
  17.9 63.2 reduce-scatter.1
where the time goes:
time: 89.8 us; the launch traced here: 89.6 us
  waiting for transfers between devices  63.4 us (71%)
  between operations  13.4 us (15%)
  blocking collectives  7.39 us (8%)
  matrix products  3.04 us (3%)
  other arithmetic  1.51 us (2%)
    reduce_scatter x1, waiting for transfers between devices, local(): lax.psum_scatter(partial_value.astype(jnp.bfloat16), 'col', scatter_dimen...  63.4 us
    all_gather x1, blocking collectives, local(): gathered = lax.all_gather(features, 'row', axis=0, tiled=True)  7.39 us
  transfers between devices with their start and end apart: 1, of which 1 were waited for; matrix products, arithmetic and copies ran while one was open for 0% of the time, Pallas kernels for 0%

commit v1 on v0

v1 whole, which is shorter than its diff:
```python
import functools

import jax
import jax.numpy as jnp
from jax import lax
from jax.experimental import pallas as pl
from jax.experimental.pallas import tpu as pltpu
from jax.sharding import PartitionSpec as P

MESH = pl.DeviceIdType.MESH
HALVES = 2
INNER = 2


def layer_kernel(
    n_row, n_out, bs,
    feat_hbm, blocks_hbm, col_hbm, count_hbm, weight_hbm, bias_hbm, out_ref,
    feat, blocks, cols, counts, weight, bias, stripe, dense, terms, pair_in, pair_out, owner_in,
    load_sem, ag_send, ag_recv, pair_send, pair_recv, owner_send, owner_recv,
):
    row = lax.axis_index("row")
    col = lax.axis_index("col")
    outer, inner = col // INNER, col % INNER
    partner = outer * INNER + 1 - inner
    width = stripe.shape[2]
    slots = blocks.shape[1]

    def load(index, src, dst):
        copy = pltpu.make_async_copy(src, dst, load_sem.at[index])
        copy.start()
        return copy

    barrier = pltpu.get_barrier_semaphore()
    for shift in range(1, n_row):
        pl.semaphore_signal(barrier, inc=1, device_id=(lax.rem(row + shift, n_row), col), device_id_type=MESH)
    pl.semaphore_signal(barrier, inc=1, device_id=(row, partner), device_id_type=MESH)
    for shift in range(1, n_out):
        pl.semaphore_signal(
            barrier, inc=1, device_id=(row, lax.rem(outer + shift, n_out) * INNER + inner), device_id_type=MESH
        )

    feat_load = load(0, feat_hbm, feat)
    weight_load = load(1, weight_hbm, weight)
    col_load = load(2, col_hbm, cols)
    count_load = load(3, count_hbm, counts)
    block_load = load(4, blocks_hbm, blocks)
    bias_load = load(5, bias_hbm, bias)

    def owner_of(i):
        down = n_out - 1 - i
        down = down - (down <= outer).astype(jnp.int32)
        up = i + (i >= outer).astype(jnp.int32)
        low = (outer < n_out // 2).astype(jnp.int32)
        last = jnp.where(i == n_out - 1, 1, 0)
        return last * outer + (1 - last) * (low * down + (1 - low) * up)

    feat_load.wait()
    weight_load.wait()
    own_rows = pl.ds(pl.multiple_of(row * bs, bs), bs)
    product = jnp.dot(feat[...], weight[...], preferred_element_type=jnp.float32).astype(jnp.bfloat16)
    for half in range(HALVES):
        stripe[half, own_rows, :] = product[:, half * width:(half + 1) * width]

    pl.semaphore_wait(barrier, n_row - 1 + 1 + n_out - 1)

    gathers = []
    for half in range(HALVES):
        for shift in range(1, n_row):
            copy = pltpu.make_async_remote_copy(
                src_ref=stripe.at[half, own_rows, :],
                dst_ref=stripe.at[half, own_rows, :],
                send_sem=ag_send.at[half, shift - 1],
                recv_sem=ag_recv.at[half, shift - 1],
                device_id=(lax.rem(row + shift, n_row), col),
                device_id_type=MESH,
            )
            copy.start()
            gathers.append(copy)

    col_load.wait()
    count_load.wait()
    block_load.wait()

    def build(slot, carry):
        group, i = slot // n_out, slot % n_out
        target = owner_of(i) * INNER + (1 - group) * (1 - inner) + group * inner
        rows = pl.ds(pl.multiple_of(slot * bs, bs), bs)
        count = counts[0, target]
        parts = [blocks[target, k].astype(jnp.float32) for k in range(slots)]
        for j in range(n_row):
            total = None
            for k in range(slots):
                live = jnp.logical_and(cols[k, target] == j, k < count)
                piece = parts[k] * jnp.where(live, 1.0, 0.0).astype(jnp.float32)
                total = piece if total is None else total + piece
            dense[rows, j * bs:(j + 1) * bs] = total.astype(jnp.bfloat16)
        return carry

    lax.fori_loop(0, INNER * n_out, build, 0)

    step = 4 if n_out % 4 == 0 else 1

    def multiply(half, group):
        def some(index, carry):
            first = group * n_out + index * step
            rows = pl.ds(pl.multiple_of(first * bs, bs), step * bs)
            value = jnp.dot(dense[rows, :], stripe[half], preferred_element_type=jnp.float32)
            terms[half, rows, :] = value.astype(jnp.bfloat16)
            return carry

        if n_out == step:
            some(0, 0)
        else:
            lax.fori_loop(0, n_out // step, some, 0)

    pairs = []
    for half in range(HALVES):
        for shift in range(1, n_row):
            gathers[half * (n_row - 1) + shift - 1].wait_recv()
        multiply(half, 0)
        for i in range(n_out):
            copy = pltpu.make_async_remote_copy(
                src_ref=terms.at[half, pl.ds(i * bs, bs), :],
                dst_ref=pair_in.at[half, i],
                send_sem=pair_send.at[half, i],
                recv_sem=pair_recv.at[half, i],
                device_id=(row, partner),
                device_id_type=MESH,
            )
            copy.start()
            pairs.append(copy)
        multiply(half, 1)

    owners, mine = [], []
    for half in range(HALVES):
        for i in range(n_out):
            pairs[half * n_out + i].wait_recv()
            first = (n_out + i) * bs
            total = terms[half, first:first + bs, :].astype(jnp.float32) + pair_in[half, i].astype(jnp.float32)
            if i == n_out - 1:
                mine.append(total)
                continue
            pair_out[half, i] = total.astype(jnp.bfloat16)
            target = owner_of(i)
            shift = lax.rem(target - outer + n_out, n_out) - 1
            copy = pltpu.make_async_remote_copy(
                src_ref=pair_out.at[half, i],
                dst_ref=owner_in.at[half, shift],
                send_sem=owner_send.at[half, i],
                recv_sem=owner_recv.at[half, shift],
                device_id=(row, target * INNER + inner),
                device_id_type=MESH,
            )
            copy.start()
            owners.append(copy)

    bias_load.wait()
    for half in range(HALVES):
        total = mine[half]
        for shift in range(n_out - 1):
            pltpu.make_async_remote_copy(
                src_ref=pair_out.at[half, 0],
                dst_ref=owner_in.at[half, shift],
                send_sem=owner_send.at[half, 0],
                recv_sem=owner_recv.at[half, shift],
                device_id=(row, partner),
                device_id_type=MESH,
            ).wait_recv()
            total = total + owner_in[half, shift].astype(jnp.float32)
        span = slice(half * width, (half + 1) * width)
        out_ref[:, span] = jnp.maximum(total + bias[:, span], 0.0).astype(jnp.bfloat16)

    for copy in gathers + pairs + owners:
        copy.wait_send()


def local(n_row, n_col, features, blocks, block_col, row_count, weight, out_bias):
    bs, feat_width = blocks.shape[2], features.shape[1]
    n_out = n_col // INNER
    width = feat_width // HALVES
    bf16 = jnp.bfloat16
    return pl.pallas_call(
        functools.partial(layer_kernel, n_row, n_out, bs),
        out_shape=jax.ShapeDtypeStruct(features.shape, bf16),
        in_specs=[pl.BlockSpec(memory_space=pltpu.HBM)] * 6,
        out_specs=pl.BlockSpec(memory_space=pltpu.VMEM),
        scratch_shapes=[
            pltpu.VMEM(features.shape, bf16),
            pltpu.VMEM(blocks.shape, bf16),
            pltpu.SMEM(block_col.shape[::-1], jnp.int32),
            pltpu.SMEM(row_count.shape[::-1], jnp.int32),
            pltpu.VMEM(weight.shape, bf16),
            pltpu.VMEM((1, feat_width), jnp.float32),
            pltpu.VMEM((HALVES, n_row * bs, width), bf16),
            pltpu.VMEM((n_col * bs, n_row * bs), bf16),
            pltpu.VMEM((HALVES, n_col * bs, width), bf16),
            pltpu.VMEM((HALVES, n_out, bs, width), bf16),
            pltpu.VMEM((HALVES, n_out - 1, bs, width), bf16),
            pltpu.VMEM((HALVES, n_out - 1, bs, width), bf16),
            pltpu.SemaphoreType.DMA((6,)),
            pltpu.SemaphoreType.DMA((HALVES, n_row - 1)),
            pltpu.SemaphoreType.DMA((HALVES, n_row - 1)),
            pltpu.SemaphoreType.DMA((HALVES, n_out)),
            pltpu.SemaphoreType.DMA((HALVES, n_out)),
            pltpu.SemaphoreType.DMA((HALVES, n_out - 1)),
            pltpu.SemaphoreType.DMA((HALVES, n_out - 1)),
        ],
        compiler_params=pltpu.CompilerParams(
            collective_id=0, has_side_effects=True, vmem_limit_bytes=52 * 1024 * 1024
        ),
    )(features, blocks, block_col.T, row_count.T, weight, out_bias.reshape(1, feat_width))


def solution(mesh):
    return jax.shard_map(
        functools.partial(local, mesh.shape["row"], mesh.shape["col"]),
        mesh=mesh,
        in_specs=(
            P(("row", "col"), None),
            P("row", "col", None, None),
            P("row", "col"),
            P("row", "col"),
            P(),
            P(),
        ),
        out_specs=P(("row", "col"), None),
        check_vma=False,
    )
```

time: 89.8 us -> 24.4 us (0.27)
  waiting for transfers between devices: 63.4 us -> 0 us
  Pallas kernels: 0 us -> 19.8 us
  between operations: 13.4 us -> 0.02 us
  blocking collectives: 7.39 us -> 0 us
  local copies, waits for them, and re-layouts: 0.86 us -> 4.29 us
  matrix products: 3.04 us -> 0 us
  other arithmetic: 1.51 us -> 0 us
    reduce_scatter x1 -> x0, waiting for transfers between devices: 63.4 us -> none  [local(): lax.psum_scatter(partial_value.astype(jnp.bfloat16), 'col', scatter_dimen...]
    pallas_call x0 -> x1, Pallas kernels: none -> 19.8 us  [local(): pl.pallas_call(functools.partial(layer_kernel, n_row, n_out, bs), out_sha...]
    all_gather x1 -> x0, blocking collectives: 7.39 us -> none  [local(): gathered = lax.all_gather(features, 'row', axis=0, tiled=True)]
    unnamed x6 -> x13, local copies, waits for them, and re-layouts: 0.02 us -> 4.29 us
    dot_general x2 -> x0, matrix products: 3.04 us -> none  [the longest x1 1.64 us: local(): jnp.dot(summed, weight, preferred_element_type=jnp.float32) + out_bias]
  transfers between devices with their start and end apart: 1 -> 0, of which waited for: 1 -> 0; matrix products, arithmetic and copies ran while one was open for 0% -> 0% of each run, Pallas kernels for 0% -> 0%
where the time goes in v1:
time: 24.4 us; the launch traced here: 24.1 us
  Pallas kernels  19.8 us (81%)
  local copies, waits for them, and re-layouts  4.29 us (18%)
    pallas_call x1, Pallas kernels, local(): pl.pallas_call(functools.partial(layer_kernel, n_row, n_out, bs), out_sha...  19.8 us
    unnamed x13, local copies, waits for them, and re-layouts  4.29 us

profile of v1, /device:TPU:0, one launch (start us, length us, event | category | flops | bytes accessed | tf_op | source)
XLA Modules:
  0.0 24.1 jit_solution(9922854194013773406)
XLA Ops:
  0.0 0.0 copy-start.3
  0.0 0.0 copy-start.4
  0.0 0.0 copy-start.5
  0.0 0.7 %copy-done.3 = s32[8,4]{0,1:T(4,128)S(1)} copy-done((s32[8,4]{0,1:T(4,128)S(1)}, s32[8,4]{0,1:T(4,128)}, u32[]{:S(2)}) %copy-start.3) | copy-done | bytes 152
  0.7 0.0 copy-done.4
  0.7 0.0 copy-done.5
  0.7 0.0 copy-start
  0.7 1.2 %copy-done = bf16[8,4,128,128]{3,2,1,0:T(8,128)(2,1)S(1)} copy-done((bf16[8,4,128,128]{3,2,1,0:T(8,128)(2,1)S(1)}, bf16[8,4,128,128]{3,2,1,0:T(8,128)(2,1)}, u32[]{:S(2)}) %copy-start) | copy-done | bytes 1048600
  1.9 0.0 copy-start.1
  1.9 0.9 %copy-done.1 = bf16[256,256]{1,0:T(8,128)(2,1)S(1)} copy-done((bf16[256,256]{1,0:T(8,128)(2,1)S(1)}, bf16[256,256]{1,0:T(8,128)(2,1)}, u32[]{:S(2)}) %copy-start.1) | copy-done | bytes 131096
  2.8 0.0 copy-start.2
  2.8 0.8 %copy-done.2 = bf16[128,256]{1,0:T(8,128)(2,1)S(1)} copy-done((bf16[128,256]{1,0:T(8,128)(2,1)S(1)}, bf16[128,256]{1,0:T(8,128)(2,1)}, u32[]{:S(2)}) %copy-start.2) | copy-done | bytes 65560
  3.7 19.8 %shard_map.64 = bf16[128,256]{1,0:T(8,128)(2,1)S(1)} custom-call(bf16[128,256]{1,0:T(8,128)(2,1)S(1)} %copy-done.2, bf16[8,4,128,128]{3,2,1,0:T(8,128)(2,1)S(1)} %copy-done, s32[4,8]{1,0:T(4,128)S(1)} %bitcast.3, s32[1,8]{1,0:T(1,128)S(1)} %bitcast.5, bf16[256,256]{1,0:T(8,128)(2,1)S(1)} %copy-done.1, f32[1,256]{1,0:T(1,128)S(1)} %bitcast.4), custom_call_target="tpu_custom_call" | custom-call | tf_op jit(solution)/shard_map/pallas_call | solution.py:182
  23.5 0.6 %copy.8 = bf16[128,256]{1,0:T(8,128)(2,1)} copy(bf16[128,256]{1,0:T(8,128)(2,1)S(1)} %shard_map.64) | data formatting | bytes 131072
Async XLA Ops:
  0.0 0.7 %copy-start.3 = (s32[8,4]{0,1:T(4,128)S(1)}, s32[8,4]{0,1:T(4,128)}, u32[]{:S(2)}) copy-start(s32[8,4]{0,1:T(4,128)} %param.8) | copy-start | bytes 388
  0.0 0.7 %copy-start.4 = (f32[256]{0:T(256)S(1)}, f32[256]{0:T(256)}, u32[]{:S(2)}) copy-start(f32[256]{0:T(256)} %param.11) | copy-start | bytes 3076
  0.0 0.7 %copy-start.5 = (s32[8,1]{0,1:T(1,128)S(1)}, s32[8,1]{0,1:T(1,128)}, u32[]{:S(2)}) copy-start(s32[8,1]{0,1:T(1,128)} %param.9) | copy-start | bytes 100
  0.7 1.2 %copy-start = (bf16[8,4,128,128]{3,2,1,0:T(8,128)(2,1)S(1)}, bf16[8,4,128,128]{3,2,1,0:T(8,128)(2,1)}, u32[]{:S(2)}) copy-start(bf16[8,4,128,128]{3,2,1,0:T(8,128)(2,1)} %blocks_hbm.1) | copy-start | bytes 3145732
  1.9 0.9 %copy-start.1 = (bf16[256,256]{1,0:T(8,128)(2,1)S(1)}, bf16[256,256]{1,0:T(8,128)(2,1)}, u32[]{:S(2)}) copy-start(bf16[256,256]{1,0:T(8,128)(2,1)} %weight_hbm.1) | copy-start | bytes 393220
  2.8 0.8 %copy-start.2 = (bf16[128,256]{1,0:T(8,128)(2,1)S(1)}, bf16[128,256]{1,0:T(8,128)(2,1)}, u32[]{:S(2)}) copy-start(bf16[128,256]{1,0:T(8,128)(2,1)} %feat_hbm.1) | copy-start | bytes 196612

commit v2 on v1

--- a/solution.py
+++ b/solution.py
@@ -15,7 +15,7 @@
 def layer_kernel(
     n_row, n_out, bs,
     feat_hbm, blocks_hbm, col_hbm, count_hbm, weight_hbm, bias_hbm, out_ref,
-    feat, blocks, cols, counts, weight, bias, stripe, dense, terms, pair_in, pair_out, owner_in,
+    blocks, cols, counts, weight, bias, stripe, dense, terms, pair_in, pair_out, owner_in,
     load_sem, ag_send, ag_recv, pair_send, pair_recv, owner_send, owner_recv,
 ):
     row = lax.axis_index("row")
@@ -39,12 +39,17 @@
             barrier, inc=1, device_id=(row, lax.rem(outer + shift, n_out) * INNER + inner), device_id_type=MESH
         )
 
-    feat_load = load(0, feat_hbm, feat)
-    weight_load = load(1, weight_hbm, weight)
-    col_load = load(2, col_hbm, cols)
-    count_load = load(3, count_hbm, counts)
-    block_load = load(4, blocks_hbm, blocks)
-    bias_load = load(5, bias_hbm, bias)
+    own_rows = pl.ds(pl.multiple_of(row * bs, bs), bs)
+
+    def own_half(half):
+        return feat_hbm.at[:, half * width:(half + 1) * width]
+
+    block_load = load(0, blocks_hbm, blocks)
+    col_load = load(1, col_hbm, cols)
+    count_load = load(2, count_hbm, counts)
+    own_loads = [load(5 + half, own_half(half), stripe.at[half, own_rows, :]) for half in range(HALVES)]
+    weight_load = load(3, weight_hbm, weight)
+    bias_load = load(4, bias_hbm, bias)
 
     def owner_of(i):
         down = n_out - 1 - i
@@ -54,20 +59,13 @@
         last = jnp.where(i == n_out - 1, 1, 0)
         return last * outer + (1 - last) * (low * down + (1 - low) * up)
 
-    feat_load.wait()
-    weight_load.wait()
-    own_rows = pl.ds(pl.multiple_of(row * bs, bs), bs)
-    product = jnp.dot(feat[...], weight[...], preferred_element_type=jnp.float32).astype(jnp.bfloat16)
-    for half in range(HALVES):
-        stripe[half, own_rows, :] = product[:, half * width:(half + 1) * width]
-
     pl.semaphore_wait(barrier, n_row - 1 + 1 + n_out - 1)
 
     gathers = []
     for half in range(HALVES):
         for shift in range(1, n_row):
             copy = pltpu.make_async_remote_copy(
-                src_ref=stripe.at[half, own_rows, :],
+                src_ref=own_half(half),
                 dst_ref=stripe.at[half, own_rows, :],
                 send_sem=ag_send.at[half, shift - 1],
                 recv_sem=ag_recv.at[half, shift - 1],
@@ -113,34 +111,41 @@
         else:
             lax.fori_loop(0, n_out // step, some, 0)
 
-    pairs = []
-    for half in range(HALVES):
+    pairs = {}
+
+    def send_pair(half, i):
+        copy = pltpu.make_async_remote_copy(
+            src_ref=terms.at[half, pl.ds(i * bs, bs), :],
+            dst_ref=pair_in.at[half, i],
+            send_sem=pair_send.at[half, i],
+            recv_sem=pair_recv.at[half, i],
+            device_id=(row, partner),
+            device_id_type=MESH,
+        )
+        copy.start()
+        pairs[half, i] = copy
+
+    for half in range(HALVES):
+        own_loads[half].wait()
         for shift in range(1, n_row):
             gathers[half * (n_row - 1) + shift - 1].wait_recv()
         multiply(half, 0)
-        for i in range(n_out):
-            copy = pltpu.make_async_remote_copy(
-                src_ref=terms.at[half, pl.ds(i * bs, bs), :],
-                dst_ref=pair_in.at[half, i],
-                send_sem=pair_send.at[half, i],
-                recv_sem=pair_recv.at[half, i],
-                device_id=(row, partner),
-                device_id_type=MESH,
-            )
-            copy.start()
-            pairs.append(copy)
+        for i in range(n_out - 1):
+            send_pair(half, i)
+        if half == HALVES - 1:
+            for other in range(HALVES):
+                send_pair(other, n_out - 1)
         multiply(half, 1)
 
-    owners, mine = [], []
-    for half in range(HALVES):
-        for i in range(n_out):
-            pairs[half * n_out + i].wait_recv()
-            first = (n_out + i) * bs
-            total = terms[half, first:first + bs, :].astype(jnp.float32) + pair_in[half, i].astype(jnp.float32)
-            if i == n_out - 1:
-                mine.append(total)
-                continue
-            pair_out[half, i] = total.astype(jnp.bfloat16)
+    def pair_sum(half, i):
+        pairs[half, i].wait_recv()
+        first = (n_out + i) * bs
+        return terms[half, first:first + bs, :].astype(jnp.float32) + pair_in[half, i].astype(jnp.float32)
+
+    owners = []
+    for half in range(HALVES):
+        for i in range(n_out - 1):
+            pair_out[half, i] = pair_sum(half, i).astype(jnp.bfloat16)
             target = owner_of(i)
             shift = lax.rem(target - outer + n_out, n_out) - 1
             copy = pltpu.make_async_remote_copy(
@@ -153,8 +158,11 @@
             )
             copy.start()
             owners.append(copy)
+    mine = [pair_sum(half, n_out - 1) for half in range(HALVES)]
 
     bias_load.wait()
+    weight_load.wait()
+    hidden = bias[...]
     for half in range(HALVES):
         total = mine[half]
         for shift in range(n_out - 1):
@@ -168,9 +176,10 @@
             ).wait_recv()
             total = total + owner_in[half, shift].astype(jnp.float32)
         span = slice(half * width, (half + 1) * width)
-        out_ref[:, span] = jnp.maximum(total + bias[:, span], 0.0).astype(jnp.bfloat16)
-
-    for copy in gathers + pairs + owners:
+        hidden = hidden + jnp.dot(total.astype(jnp.bfloat16), weight[span, :], preferred_element_type=jnp.float32)
+    out_ref[...] = jnp.maximum(hidden, 0.0).astype(jnp.bfloat16)
+
+    for copy in gathers + list(pairs.values()) + owners:
         copy.wait_send()
 
 
@@ -185,7 +194,6 @@
         in_specs=[pl.BlockSpec(memory_space=pltpu.HBM)] * 6,
         out_specs=pl.BlockSpec(memory_space=pltpu.VMEM),
         scratch_shapes=[
-            pltpu.VMEM(features.shape, bf16),
             pltpu.VMEM(blocks.shape, bf16),
             pltpu.SMEM(block_col.shape[::-1], jnp.int32),
             pltpu.SMEM(row_count.shape[::-1], jnp.int32),
@@ -197,7 +205,7 @@
             pltpu.VMEM((HALVES, n_out, bs, width), bf16),
             pltpu.VMEM((HALVES, n_out - 1, bs, width), bf16),
             pltpu.VMEM((HALVES, n_out - 1, bs, width), bf16),
-            pltpu.SemaphoreType.DMA((6,)),
+            pltpu.SemaphoreType.DMA((5 + HALVES,)),
             pltpu.SemaphoreType.DMA((HALVES, n_row - 1)),
             pltpu.SemaphoreType.DMA((HALVES, n_row - 1)),
             pltpu.SemaphoreType.DMA((HALVES, n_out)),
@@ -206,7 +214,7 @@
             pltpu.SemaphoreType.DMA((HALVES, n_out - 1)),
         ],
         compiler_params=pltpu.CompilerParams(
-            collective_id=0, has_side_effects=True, vmem_limit_bytes=52 * 1024 * 1024
+            collective_id=0, has_side_effects=True, vmem_limit_bytes=58 * 1024 * 1024
         ),
     )(features, blocks, block_col.T, row_count.T, weight, out_bias.reshape(1, feat_width))
 

time: 24.4 us -> 22.2 us (0.910)
  local copies, waits for them, and re-layouts: 4.29 us -> 1.47 us
  Pallas kernels: 19.8 us -> 20.5 us
    unnamed x13 -> x1, local copies, waits for them, and re-layouts: 4.29 us -> 1.47 us
    pallas_call x1, Pallas kernels: 19.8 us -> 20.5 us  [local(): pl.pallas_call(functools.partial(layer_kernel, n_row, n_out, bs), out_sha...]
where the time goes in v2:
time: 22.2 us; the launch traced here: 22 us
  Pallas kernels  20.5 us (92%)
  local copies, waits for them, and re-layouts  1.47 us (7%)
    pallas_call x1, Pallas kernels, local(): pl.pallas_call(functools.partial(layer_kernel, n_row, n_out, bs), out_sha...  20.5 us
    unnamed x1, local copies, waits for them, and re-layouts  1.47 us

profile of v2, /device:TPU:0, one launch (start us, length us, event | category | flops | bytes accessed | tf_op | source)
XLA Modules:
  0.0 22.0 jit_solution(10471867505932332949)
XLA Ops:
  0.0 20.5 %shard_map.64 = bf16[128,256]{1,0:T(8,128)(2,1)} custom-call(bf16[128,256]{1,0:T(8,128)(2,1)} %feat_hbm.1, bf16[8,4,128,128]{3,2,1,0:T(8,128)(2,1)} %blocks_hbm.1, s32[4,8]{1,0:T(4,128)} %bitcast.3, s32[1,8]{1,0:T(1,128)} %bitcast.5, bf16[256,256]{1,0:T(8,128)(2,1)} %weight_hbm.1, f32[1,256]{1,0:T(1,128)} %bitcast.4), custom_call_target="tpu_custom_call" | custom-call | tf_op jit(solution)/shard_map/pallas_call | solution.py:191
  20.6 1.5 %copy.8 = bf16[128,256]{1,0:T(8,128)(2,1)} copy(bf16[128,256]{1,0:T(8,128)(2,1)} %shard_map.64) | data formatting | bytes 131072

commit v3 on v2

--- a/solution.py
+++ b/solution.py
@@ -39,18 +39,6 @@
             barrier, inc=1, device_id=(row, lax.rem(outer + shift, n_out) * INNER + inner), device_id_type=MESH
         )
 
-    own_rows = pl.ds(pl.multiple_of(row * bs, bs), bs)
-
-    def own_half(half):
-        return feat_hbm.at[:, half * width:(half + 1) * width]
-
-    block_load = load(0, blocks_hbm, blocks)
-    col_load = load(1, col_hbm, cols)
-    count_load = load(2, count_hbm, counts)
-    own_loads = [load(5 + half, own_half(half), stripe.at[half, own_rows, :]) for half in range(HALVES)]
-    weight_load = load(3, weight_hbm, weight)
-    bias_load = load(4, bias_hbm, bias)
-
     def owner_of(i):
         down = n_out - 1 - i
         down = down - (down <= outer).astype(jnp.int32)
@@ -58,6 +46,27 @@
         low = (outer < n_out // 2).astype(jnp.int32)
         last = jnp.where(i == n_out - 1, 1, 0)
         return last * outer + (1 - last) * (low * down + (1 - low) * up)
+
+    own_rows = pl.ds(pl.multiple_of(row * bs, bs), bs)
+
+    def own_half(half):
+        return feat_hbm.at[:, half * width:(half + 1) * width]
+
+    def target_of(group, i):
+        return owner_of(i) * INNER + (inner if group else 1 - inner)
+
+    col_load = load(0, col_hbm, cols)
+    count_load = load(1, count_hbm, counts)
+    block_loads = {}
+    for group in range(INNER):
+        for i in range(n_out):
+            slot = group * n_out + i
+            block_loads[group, i] = load(4 + HALVES + slot, blocks_hbm.at[target_of(group, i)], blocks.at[slot])
+        if group == 0:
+            own_loads = [load(4 + half, own_half(half), stripe.at[half, own_rows, :]) for half in range(HALVES)]
+    weight_load = load(2, weight_hbm, weight)
+    bias_load = load(3, bias_hbm, bias)
+
 
     pl.semaphore_wait(barrier, n_row - 1 + 1 + n_out - 1)
 
@@ -77,25 +86,30 @@
 
     col_load.wait()
     count_load.wait()
-    block_load.wait()
-
-    def build(slot, carry):
-        group, i = slot // n_out, slot % n_out
-        target = owner_of(i) * INNER + (1 - group) * (1 - inner) + group * inner
-        rows = pl.ds(pl.multiple_of(slot * bs, bs), bs)
-        count = counts[0, target]
-        parts = [blocks[target, k].astype(jnp.float32) for k in range(slots)]
-        for j in range(n_row):
-            total = None
-            for k in range(slots):
-                live = jnp.logical_and(cols[k, target] == j, k < count)
-                piece = parts[k] * jnp.where(live, 1.0, 0.0).astype(jnp.float32)
-                total = piece if total is None else total + piece
-            dense[rows, j * bs:(j + 1) * bs] = total.astype(jnp.bfloat16)
-        return carry
-
-    lax.fori_loop(0, INNER * n_out, build, 0)
-
+
+    def build(group):
+        for i in range(n_out):
+            block_loads[group, i].wait()
+            slot, target = group * n_out + i, target_of(group, i)
+            count = counts[0, target]
+            live_cols = [jnp.where(k < count, cols[k, target], -1) for k in range(slots)]
+
+            def column(j, carry):
+                total = None
+                for k in range(slots):
+                    part = blocks[slot, k]
+                    piece = jnp.where(live_cols[k] == j, part, jnp.zeros_like(part))
+                    total = piece if total is None else total + piece
+                dense[slot * bs:(slot + 1) * bs, pl.ds(pl.multiple_of(j * bs, bs), bs)] = total
+                return carry
+
+            if n_row <= 4:
+                for j in range(n_row):
+                    column(j, 0)
+            else:
+                lax.fori_loop(0, n_row, column, 0)
+
+    build(0)
     step = 4 if n_out % 4 == 0 else 1
 
     def multiply(half, group):
@@ -125,6 +139,28 @@
         copy.start()
         pairs[half, i] = copy
 
+    def pair_sum(half, i):
+        pairs[half, i].wait_recv()
+        first = (n_out + i) * bs
+        return terms[half, first:first + bs, :].astype(jnp.float32) + pair_in[half, i].astype(jnp.float32)
+
+    owners = []
+
+    def send_owner(half, i):
+        pair_out[half, i] = pair_sum(half, i).astype(jnp.bfloat16)
+        target = owner_of(i)
+        shift = lax.rem(target - outer + n_out, n_out) - 1
+        copy = pltpu.make_async_remote_copy(
+            src_ref=pair_out.at[half, i],
+            dst_ref=owner_in.at[half, shift],
+            send_sem=owner_send.at[half, i],
+            recv_sem=owner_recv.at[half, shift],
+            device_id=(row, target * INNER + inner),
+            device_id_type=MESH,
+        )
+        copy.start()
+        owners.append(copy)
+
     for half in range(HALVES):
         own_loads[half].wait()
         for shift in range(1, n_row):
@@ -132,32 +168,16 @@
         multiply(half, 0)
         for i in range(n_out - 1):
             send_pair(half, i)
-        if half == HALVES - 1:
-            for other in range(HALVES):
-                send_pair(other, n_out - 1)
-        multiply(half, 1)
-
-    def pair_sum(half, i):
-        pairs[half, i].wait_recv()
-        first = (n_out + i) * bs
-        return terms[half, first:first + bs, :].astype(jnp.float32) + pair_in[half, i].astype(jnp.float32)
-
-    owners = []
-    for half in range(HALVES):
+        if half == 0:
+            build(1)
+            multiply(half, 1)
+    for half in range(HALVES):
+        send_pair(half, n_out - 1)
+    for half in range(HALVES):
+        if half:
+            multiply(half, 1)
         for i in range(n_out - 1):
-            pair_out[half, i] = pair_sum(half, i).astype(jnp.bfloat16)
-            target = owner_of(i)
-            shift = lax.rem(target - outer + n_out, n_out) - 1
-            copy = pltpu.make_async_remote_copy(
-                src_ref=pair_out.at[half, i],
-                dst_ref=owner_in.at[half, shift],
-                send_sem=owner_send.at[half, i],
-                recv_sem=owner_recv.at[half, shift],
-                device_id=(row, target * INNER + inner),
-                device_id_type=MESH,
-            )
-            copy.start()
-            owners.append(copy)
+            send_owner(half, i)
     mine = [pair_sum(half, n_out - 1) for half in range(HALVES)]
 
     bias_load.wait()
@@ -205,7 +225,7 @@
             pltpu.VMEM((HALVES, n_out, bs, width), bf16),
             pltpu.VMEM((HALVES, n_out - 1, bs, width), bf16),
             pltpu.VMEM((HALVES, n_out - 1, bs, width), bf16),
-            pltpu.SemaphoreType.DMA((5 + HALVES,)),
+            pltpu.SemaphoreType.DMA((4 + HALVES + n_col,)),
             pltpu.SemaphoreType.DMA((HALVES, n_row - 1)),
             pltpu.SemaphoreType.DMA((HALVES, n_row - 1)),
             pltpu.SemaphoreType.DMA((HALVES, n_out)),

time: 22.2 us -> 22.2 us (level)
  no operation moved by 1% of the time
where the time goes in v3:
time: 22.2 us; the launch traced here: 22.1 us
  Pallas kernels  20.6 us (93%)
  local copies, waits for them, and re-layouts  1.47 us (7%)
    pallas_call x1, Pallas kernels, local(): pl.pallas_call(functools.partial(layer_kernel, n_row, n_out, bs), out_sha...  20.6 us
    unnamed x1, local copies, waits for them, and re-layouts  1.47 us

profile of v3, /device:TPU:0, one launch (start us, length us, event | category | flops | bytes accessed | tf_op | source)
XLA Modules:
  0.0 22.1 jit_solution(9382526436250390777)
XLA Ops:
  0.0 20.6 %shard_map.64 = bf16[128,256]{1,0:T(8,128)(2,1)} custom-call(bf16[128,256]{1,0:T(8,128)(2,1)} %feat_hbm.1, bf16[8,4,128,128]{3,2,1,0:T(8,128)(2,1)} %blocks_hbm.1, s32[4,8]{1,0:T(4,128)} %bitcast.3, s32[1,8]{1,0:T(1,128)} %bitcast.5, bf16[256,256]{1,0:T(8,128)(2,1)} %weight_hbm.1, f32[1,256]{1,0:T(1,128)} %bitcast.4), custom_call_target="tpu_custom_call" | custom-call | tf_op jit(solution)/shard_map/pallas_call | solution.py:211
  20.6 1.5 %copy.8 = bf16[128,256]{1,0:T(8,128)(2,1)} copy(bf16[128,256]{1,0:T(8,128)(2,1)} %shard_map.64) | data formatting | bytes 131072

commit v4 on v3

--- a/solution.py
+++ b/solution.py
@@ -210,7 +210,7 @@
     bf16 = jnp.bfloat16
     return pl.pallas_call(
         functools.partial(layer_kernel, n_row, n_out, bs),
-        out_shape=jax.ShapeDtypeStruct(features.shape, bf16),
+        out_shape=pltpu.VMEM(features.shape, bf16),
         in_specs=[pl.BlockSpec(memory_space=pltpu.HBM)] * 6,
         out_specs=pl.BlockSpec(memory_space=pltpu.VMEM),
         scratch_shapes=[

time: 22.2 us -> 20.8 us (0.937)
  local copies, waits for them, and re-layouts: 1.47 us -> 0.63 us
  Pallas kernels: 20.6 us -> 20 us
    unnamed x1, local copies, waits for them, and re-layouts: 1.47 us -> 0.63 us
    pallas_call x1, Pallas kernels: 20.6 us -> 20 us  [local(): pl.pallas_call(functools.partial(layer_kernel, n_row, n_out, bs), out_sha...]
where the time goes in v4:
time: 20.8 us; the launch traced here: 20.6 us
  Pallas kernels  20 us (96%)
  local copies, waits for them, and re-layouts  0.63 us (3%)
    pallas_call x1, Pallas kernels, local(): pl.pallas_call(functools.partial(layer_kernel, n_row, n_out, bs), out_sha...  20 us
    unnamed x1, local copies, waits for them, and re-layouts  0.63 us

profile of v4, /device:TPU:0, one launch (start us, length us, event | category | flops | bytes accessed | tf_op | source)
XLA Modules:
  0.0 20.6 jit_solution(5689289509308320255)
XLA Ops:
  0.0 20.0 %shard_map.64 = bf16[128,256]{1,0:T(8,128)(2,1)S(1)} custom-call(bf16[128,256]{1,0:T(8,128)(2,1)} %feat_hbm.1, bf16[8,4,128,128]{3,2,1,0:T(8,128)(2,1)} %blocks_hbm.1, s32[4,8]{1,0:T(4,128)} %bitcast.3, s32[1,8]{1,0:T(1,128)} %bitcast.5, bf16[256,256]{1,0:T(8,128)(2,1)} %weight_hbm.1, f32[1,256]{1,0:T(1,128)} %bitcast.4), custom_call_target="tpu_custom_call" | custom-call | tf_op jit(solution)/shard_map/pallas_call | solution.py:211
  20.0 0.6 %copy.8 = bf16[128,256]{1,0:T(8,128)(2,1)} copy(bf16[128,256]{1,0:T(8,128)(2,1)S(1)} %shard_map.64) | data formatting | bytes 131072

commit v5 on v4

--- a/solution.py
+++ b/solution.py
@@ -165,9 +165,12 @@
         own_loads[half].wait()
         for shift in range(1, n_row):
             gathers[half * (n_row - 1) + shift - 1].wait_recv()
-        multiply(half, 0)
-        for i in range(n_out - 1):
-            send_pair(half, i)
+        for first in range(0, n_out, INNER):
+            rows = slice(first * bs, (first + INNER) * bs)
+            value = jnp.dot(dense[rows, :], stripe[half], preferred_element_type=jnp.float32)
+            terms[half, rows, :] = value.astype(jnp.bfloat16)
+            for i in range(first, min(first + INNER, n_out - 1)):
+                send_pair(half, i)
         if half == 0:
             build(1)
             multiply(half, 1)

time: 20.8 us -> 20.6 us (level)
  no operation moved by 1% of the time
where the time goes in v5:
time: 20.6 us; the launch traced here: 20.5 us
  Pallas kernels  19.8 us (96%)
  local copies, waits for them, and re-layouts  0.63 us (3%)
    pallas_call x1, Pallas kernels, local(): pl.pallas_call(functools.partial(layer_kernel, n_row, n_out, bs), out_sha...  19.8 us
    unnamed x1, local copies, waits for them, and re-layouts  0.63 us

profile of v5, /device:TPU:0, one launch (start us, length us, event | category | flops | bytes accessed | tf_op | source)
XLA Modules:
  0.0 20.5 jit_solution(3835635020746830701)
XLA Ops:
  0.0 19.8 %shard_map.64 = bf16[128,256]{1,0:T(8,128)(2,1)S(1)} custom-call(bf16[128,256]{1,0:T(8,128)(2,1)} %feat_hbm.1, bf16[8,4,128,128]{3,2,1,0:T(8,128)(2,1)} %blocks_hbm.1, s32[4,8]{1,0:T(4,128)} %bitcast.3, s32[1,8]{1,0:T(1,128)} %bitcast.5, bf16[256,256]{1,0:T(8,128)(2,1)} %weight_hbm.1, f32[1,256]{1,0:T(1,128)} %bitcast.4), custom_call_target="tpu_custom_call" | custom-call | tf_op jit(solution)/shard_map/pallas_call | solution.py:214
  19.8 0.6 %copy.8 = bf16[128,256]{1,0:T(8,128)(2,1)} copy(bf16[128,256]{1,0:T(8,128)(2,1)S(1)} %shard_map.64) | data formatting | bytes 131072
